TPU v7x, 32 devices: a whole 2x2x4 slice. The times are simulated.
32 devices in a mesh: groups: 2 (over y), blocks: 4 (over z), tiles: 2 (over x), sub: 2 (over core).
Axes of the slice: x: 2, y: 2, z: 4, core: 2. Of those that a mesh axis runs over, the one named last changes fastest.
Arguments:
- seg_feat: bfloat16 [8, 4, 2048, 128], P(('groups', 'tiles', 'sub'), 'blocks'), parts along dimension 0, may hold values from -6 to 6
- seg_block: int32 [8, 4, 2048, 1], P(('groups', 'tiles', 'sub'), 'blocks'), parts along dimension 0, may hold values from 0 to 3; in each aligned block of 2048 rows (0 to 2047, 2048 to 4095, ..., all dimensions but the last counted through in order) at most 1024 rows name the same one
- depth_rank: int32 [8, 4, 8, 256], P(('groups', 'tiles', 'sub'), 'blocks'), parts along dimension 0, may hold values from 0 to 7, as said below
- w_in: bfloat16 [4, 128, 512], P('blocks'), may hold values from -0.5 to 0.5
- w_hidden: bfloat16 [4, 4, 512, 512], P('blocks'), may hold values from -0.25 to 0.25
- w_out: bfloat16 [4, 512, 128], P('blocks'), may hold values from -0.25 to 0.25
- w_dens: bfloat16 [4, 512], P('blocks'), may hold values from -0.25 to 0.25
- conv_w: bfloat16 [3, 3, 3, 128, 128], replicated, may hold values from -0.1875 to 0.1875
Outputs:
- decoded: bfloat16 [128, 64, 128], P(('groups', 'tiles', 'sub'), 'blocks'), parts along dimension 0
There are 2 independent parts, one for each index of `groups`. A program takes and returns all parts, laid end to end along the dimension named above; an argument that names none is the same for every part. Nothing has to cross between parts.
Inputs may be any that keep to these rules, and one draw needn't show every extreme that they name: `seg_block`: among one device's 2048 segments, no block is named more than 1024 times; some device names some block exactly 1024 times. `depth_rank`: for every ray, its 8 segments' ranks are a permutation of 0 .. 7.
All inputs are finite; a program needn't handle non-finite values.
Results may differ from a plain program's by a relative error of at most 0.02.
Values may be sent and summed in bfloat16 or wider, within the bound.
A program may use at most 64 MiB of HBM per device.

v0:
```python
import jax
import jax.numpy as jnp
from jax import lax
from jax.sharding import PartitionSpec as P

SEGS_RAY = 8
CONV_LAYERS = 3
TW = 16
TH = 16
RAYS_DEV = 256


def with_halo(shard, sides, width):
    for axis, dim in sides:
        peers, length = (lax.axis_size(axis), shard.shape[dim])
        up = [(i, (i + 1) % peers) for i in range(peers - 1)]
        down = [(j, i) for i, j in up]
        last = lax.slice_in_dim(shard, length - width, length, axis=dim)
        initial = lax.slice_in_dim(shard, 0, width, axis=dim)
        before = lax.ppermute(last, axis, up)
        after = lax.ppermute(initial, axis, down)
        shard = jnp.concatenate([before, shard, after], axis=dim)
    return shard


def place_rows(block_ids, capacity, block_count):
    onehot = (block_ids[:, None] == jnp.arange(block_count, dtype=jnp.int32)[None, :]).astype(
        jnp.int32
    )
    before = jnp.cumsum(onehot, axis=0) - onehot
    return block_ids * capacity + jnp.sum(before * onehot, axis=1)


def evaluate(row_block, first_weight, hidden, last_weight, density_row):
    hidden_act = jax.nn.silu(
        jnp.dot(row_block, first_weight, preferred_element_type=jnp.float32)
    ).astype(jnp.bfloat16)
    for layer_index in range(hidden.shape[0]):
        update = jax.nn.silu(
            jnp.dot(hidden_act, hidden[layer_index], preferred_element_type=jnp.float32)
        )
        hidden_act = (hidden_act.astype(jnp.float32) + update).astype(jnp.bfloat16)
    features = jnp.dot(hidden_act, last_weight, preferred_element_type=jnp.float32).astype(
        jnp.bfloat16
    )
    raw_density = jnp.dot(hidden_act, density_row, preferred_element_type=jnp.float32)
    density = (0.25 * jax.nn.softplus(raw_density)).astype(jnp.bfloat16)
    return (features, density)


def composite(features, density, rank_table):
    density_f32 = density.astype(jnp.float32)
    in_front = (rank_table[:, None, :] < rank_table[None, :, :]).astype(jnp.float32)
    optical = jnp.sum(density_f32[:, None, :] * in_front, axis=0)
    weight = jnp.exp(-optical) * (1.0 - jnp.exp(-density_f32))
    pixel_color = jnp.sum(weight[:, :, None] * features.astype(jnp.float32), axis=0)
    return pixel_color.astype(jnp.bfloat16)


def conv_layer(padded, kernel, out_rows, out_cols):
    pieces = []
    for offset_y in range(3):
        for offset_x in range(3):
            pieces.append(padded[offset_y : offset_y + out_rows, offset_x : offset_x + out_cols])
    patches = jnp.concatenate(pieces, axis=-1)
    channels = kernel.shape[-1]
    result = jnp.dot(
        patches, kernel.reshape(9 * kernel.shape[2], channels), preferred_element_type=jnp.float32
    )
    center = padded[1 : 1 + out_rows, 1 : 1 + out_cols].astype(jnp.float32)
    return (center + jax.nn.silu(result)).astype(jnp.bfloat16)


def shards(seg_feat, seg_block, depth_rank, w_in, w_hidden, w_out, w_dens, conv_w):
    local_rows = seg_feat[0, 0]
    block_ids = seg_block[0, 0, :, 0]
    rank_table = depth_rank[0, 0]
    block_count = lax.axis_size("blocks")
    segments = local_rows.shape[0]
    in_width = local_rows.shape[1]
    capacity = 2 * segments // block_count
    slot_index = place_rows(block_ids, capacity, block_count)
    sendbuf = (
        jnp.zeros((block_count * capacity, in_width), jnp.bfloat16).at[slot_index].set(local_rows)
    )
    sendbuf = sendbuf.reshape(block_count, capacity, in_width)
    first_weight = w_in[0]
    hidden = w_hidden[0]
    last_weight = w_out[0]
    density_row = w_dens[0]
    out_width = last_weight.shape[1]
    received = lax.all_to_all(sendbuf, "blocks", split_axis=0, concat_axis=0, tiled=True)
    sources = received.shape[0]
    count_items = received.shape[1]
    features, density = evaluate(
        received.reshape(sources * count_items, in_width),
        first_weight,
        hidden,
        last_weight,
        density_row,
    )
    features, density = (
        features.reshape(sources, count_items, out_width),
        density.reshape(sources, count_items),
    )
    feat_back, density_back = (
        lax.all_to_all(features, "blocks", split_axis=0, concat_axis=0, tiled=True),
        lax.all_to_all(density, "blocks", split_axis=0, concat_axis=0, tiled=True),
    )
    feat_seg = feat_back.reshape(block_count * capacity, out_width)[slot_index].reshape(
        SEGS_RAY, RAYS_DEV, out_width
    )
    density_seg = density_back.reshape(block_count * capacity)[slot_index].reshape(
        SEGS_RAY, RAYS_DEV
    )
    tile_image = composite(feat_seg, density_seg, rank_table).reshape(TH, TW, out_width)
    rows_total = TH * lax.axis_size(("tiles", "sub"))
    cols_total = TW * block_count
    row_pos = (
        lax.axis_index(("tiles", "sub")) * TH
        - CONV_LAYERS
        + jnp.arange(TH + 2 * CONV_LAYERS, dtype=jnp.int32)
    )
    col_pos = (
        lax.axis_index("blocks") * TW
        - CONV_LAYERS
        + jnp.arange(TW + 2 * CONV_LAYERS, dtype=jnp.int32)
    )
    inside = ((row_pos >= 0) & (row_pos < rows_total))[:, None] & (
        (col_pos >= 0) & (col_pos < cols_total)
    )[None, :]
    current = with_halo(tile_image, (("blocks", 1), (("tiles", "sub"), 0)), CONV_LAYERS)
    for layer_index in range(CONV_LAYERS):
        margin = CONV_LAYERS - layer_index - 1
        size_h = TH + 2 * margin
        size_w = TW + 2 * margin
        current = conv_layer(current, conv_w[layer_index], size_h, size_w)
        keep_mask = inside[
            layer_index + 1 : layer_index + 1 + size_h, layer_index + 1 : layer_index + 1 + size_w
        ]
        current = jnp.where(keep_mask[:, :, None], current, jnp.zeros_like(current))
    tile_image = current
    return tile_image


def solution(mesh):
    in_specs = (
        P(("groups", "tiles", "sub"), "blocks", None, None),
        P(("groups", "tiles", "sub"), "blocks", None, None),
        P(("groups", "tiles", "sub"), "blocks", None, None),
        P("blocks", None, None),
        P("blocks", None, None, None),
        P("blocks", None, None),
        P("blocks", None),
        P(),
    )
    out_specs = P(("groups", "tiles", "sub"), "blocks", None)
    return jax.shard_map(shards, mesh=mesh, in_specs=in_specs, out_specs=out_specs, check_vma=False)
```

profile of v0, /device:TPU:1, one launch (start us, length us, event | category | flops | bytes accessed | tf_op | source)
XLA Modules:
  0.0 131.0 jit_solution(11247792190013034700)
XLA Ops:
  0.0 0.8 fusion.27
  0.8 1.1 reduce-window.6
  3.9 6.1 %scatter_custom_fusion = bf16[4096,128]{1,0:T(8,128)(2,1)S(1)} fusion(s32[2048]{0:T(1024)S(1)} %bitcast.102, bf16[1,1,2048,128]{3,2,1,0:T(8,128)(2,1)S(1)} %copy-done, bf16[]{:T(256)} %constant.53.clone.1), kind=kCustom, calls=%fused_computation.19 | custom fusion | bytes 1572866 | tf_op jit(solution)/shard_map/scatter | solution.py:84
  9.9 30.1 %all_to_all.20 = bf16[4,1024,128]{2,1,0:T(8,128)(2,1)S(1)} all-to-all(bf16[4,1024,128]{2,1,0:T(8,128)(2,1)S(1)} %bitcast.90), channel_id=1, replica_groups=mesh['groups'=2,'blocks'=4,'tiles'=2,'sub'=2] {'blocks'}, dimensions={0} | all-to-all | bytes 2097152 | tf_op jit(solution)/shard_map/all_to_all | solution.py:92
  40.0 3.6 %multiply_convert_fusion = bf16[4096,512]{1,0:T(8,128)(2,1)S(1)} fusion(bf16[4096,128]{1,0:T(8,128)(2,1)S(1)} %bitcast.92, bf16[1,128,512]{2,1,0:T(8,128)(2,1)} %param.11), kind=kOutput, calls=%fused_computation.7 | convolution fusion | flops 547356672 | bytes 5373952 | tf_op jit(solution)/shard_map/dot_general | solution.py:36
  43.6 2.3 %fusion.11 = f32[4096,512]{1,0:T(8,128)S(1)} fusion(bf16[4096,512]{1,0:T(8,128)(2,1)S(1)} %multiply_convert_fusion, bf16[1,4,512,512]{3,2,1,0:T(8,128)(2,1)S(1)} %copy-done.3), kind=kOutput, calls=%fused_computation.17 | convolution fusion | flops 2147483648 | bytes 13107200 | tf_op jit(solution)/shard_map/dot_general | solution.py:40
  46.0 6.9 %add_convert_fusion.2 = bf16[4096,512]{1,0:T(8,128)(2,1)S(1)} fusion(f32[4096,512]{1,0:T(8,128)S(1)} %fusion.11, bf16[4096,512]{1,0:T(8,128)(2,1)S(1)} %multiply_convert_fusion, bf16[1,4,512,512]{3,2,1,0:T(8,128)(2,1)S(1)} %copy-done.3), kind=kOutput, calls=%fused_computation.5 | convolution fusion | flops 2191523840 | bytes 29884416 | tf_op jit(solution)/shard_map/dot_general | solution.py:40
  52.9 2.3 %fusion.5 = f32[4096,512]{1,0:T(8,128)S(1)} fusion(bf16[4096,512]{1,0:T(8,128)(2,1)S(1)} %add_convert_fusion.2, bf16[1,4,512,512]{3,2,1,0:T(8,128)(2,1)S(1)} %copy-done.3), kind=kOutput, calls=%fused_computation.13 | convolution fusion | flops 2147483648 | bytes 13107200 | tf_op jit(solution)/shard_map/dot_general | solution.py:40
  55.2 6.9 %add_convert_fusion = bf16[4096,512]{1,0:T(8,128)(2,1)S(1)} fusion(f32[4096,512]{1,0:T(8,128)S(1)} %fusion.5, bf16[4096,512]{1,0:T(8,128)(2,1)S(1)} %add_convert_fusion.2, bf16[1,4,512,512]{3,2,1,0:T(8,128)(2,1)S(1)} %copy-done.3), kind=kOutput, calls=%fused_computation.3 | convolution fusion | flops 2191523840 | bytes 29884416 | tf_op jit(solution)/shard_map/dot_general | solution.py:40
  62.1 1.9 %copy-done.1 = bf16[4096,512]{1,0:T(8,128)(2,1)} copy-done((bf16[4096,512]{1,0:T(8,128)(2,1)}, bf16[4096,512]{1,0:T(8,128)(2,1)S(1)}, u32[]{:S(2)}) %copy-start.1) | copy-done | bytes 4194328
  64.0 1.2 fusion.30
  67.1 3.4 %all-to-all-start.1 = ((bf16[4,2,512]{2,1,0:T(2,128)(2,1)}), bf16[4,2,512]{2,1,0:T(2,128)(2,1)S(1)}, u32[]{:S(2)}, u32[]{:S(2)}) async-start(bf16[4,2,512]{2,1,0:T(2,128)(2,1)} %reshape.161), calls=%async_computation.1 | async-start | bytes 16384 | tf_op jit(solution)/shard_map/all_to_all | solution.py:108
  70.5 4.5 %convolution_convert_fusion = bf16[4096,128]{1,0:T(8,128)(2,1)} fusion(bf16[4096,512]{1,0:T(8,128)(2,1)} %copy-done.1, bf16[1,512,128]{2,1,0:T(8,128)(2,1)S(1)} %copy-done.4), kind=kOutput, calls=%fused_computation.8 | convolution fusion | flops 537395200 | bytes 5373952 | tf_op jit(solution)/shard_map/dot_general | solution.py:43
  75.0 4.4 %all-to-all-start.2 = ((bf16[4,1024,128]{2,1,0:T(8,128)(2,1)}), bf16[4,1024,128]{2,1,0:T(8,128)(2,1)S(1)}, u32[]{:S(2)}, u32[]{:S(2)}) async-start(bf16[4,1024,128]{2,1,0:T(8,128)(2,1)} %bitcast.17), calls=%async_computation.2 | async-start | bytes 2097152 | tf_op jit(solution)/shard_map/all_to_all | solution.py:107
  79.7 13.1 %gather_fusion = bf16[2048]{0:T(1024)(128)(2,1)S(1)} fusion(bf16[4096]{0:T(1024)(128)(2,1)S(1)} %bitcast.88, s32[2048]{0:T(1024)S(1)} %broadcast_clamp_fusion), kind=kCustom, calls=%fused_computation | custom fusion | bytes 16384 | tf_op jit(solution)/shard_map/gather | solution.py:113
  92.8 11.9 %all-to-all-done.2 = bf16[4,1024,128]{2,1,0:T(8,128)(2,1)S(1)} async-done(((bf16[4,1024,128]{2,1,0:T(8,128)(2,1)}), bf16[4,1024,128]{2,1,0:T(8,128)(2,1)S(1)}, u32[]{:S(2)}, u32[]{:S(2)}) %all-to-all-start.2) | async-done | bytes 1048608 | tf_op jit(solution)/shard_map/all_to_all | solution.py:107
  104.7 6.2 %gather_fusion.1 = bf16[2048,128]{1,0:T(8,128)(2,1)S(1)} fusion(bf16[4096,128]{1,0:T(8,128)(2,1)S(1)} %bitcast.89, s32[2048]{0:T(1024)S(1)} %broadcast_clamp_fusion), kind=kCustom, calls=%fused_computation.1 | custom fusion | bytes 1056768 | tf_op jit(solution)/shard_map/gather | solution.py:110
  111.3 1.3 collective-permute-start
  112.6 1.3 collective-permute-start.1
  113.9 3.2 %collective-permute-done.1 = bf16[16,3,128]{2,1,0:T(4,128)(2,1)S(1)} collective-permute-done((bf16[16,3,128]{2,1,0:T(4,128)(2,1)S(1)}, bf16[16,3,128]{2,1,0:T(4,128)(2,1)S(1)}, u32[]{:S(2)}, u32[]{:S(2)}) %collective-permute-start.1) | collective-permute-done | bytes 12320 | tf_op jit(solution)/shard_map/ppermute | solution.py:21
  117.1 5.6 %collective-permute-start.2 = (bf16[3,22,128]{2,1,0:T(8,128)(2,1)S(1)}, bf16[3,22,128]{2,1,0:T(8,128)(2,1)S(1)}, u32[]{:S(2)}, u32[]{:S(2)}) collective-permute-start(bf16[3,22,128]{2,1,0:T(8,128)(2,1)S(1)} %get-tuple-element.8), channel_id=1, source_target_pairs={{0,1},{1,2},{2,3},{4,5},{5,6},{6,7},{8,9},{9,10},{10,11},{12,13},{... | collective-permute-start | bytes 50696 | tf_op jit(solution)/shard_map/ppermute | solution.py:20
  122.7 1.9 %collective-permute-start.3 = (bf16[3,22,128]{2,1,0:T(8,128)(2,1)S(1)}, bf16[3,22,128]{2,1,0:T(8,128)(2,1)S(1)}, u32[]{:S(2)}, u32[]{:S(2)}) collective-permute-start(bf16[3,22,128]{2,1,0:T(8,128)(2,1)S(1)} %get-tuple-element.9), channel_id=1, source_target_pairs={{1,0},{2,1},{3,2},{5,4},{6,5},{7,6},{9,8},{10,9},{11,10},{13,12},{... | collective-permute-start | bytes 50696 | tf_op jit(solution)/shard_map/ppermute | solution.py:21
  124.9 2.8 %collective-permute-done.3 = bf16[3,22,128]{2,1,0:T(8,128)(2,1)S(1)} collective-permute-done((bf16[3,22,128]{2,1,0:T(8,128)(2,1)S(1)}, bf16[3,22,128]{2,1,0:T(8,128)(2,1)S(1)}, u32[]{:S(2)}, u32[]{:S(2)}) %collective-permute-start.3) | collective-permute-done | bytes 16928 | tf_op jit(solution)/shard_map/ppermute | solution.py:21
  130.0 1.0 fusion.23
  (72 shorter events, 6.9 us)
Async XLA Ops:
  0.0 3.9 %copy-start = (bf16[1,1,2048,128]{3,2,1,0:T(8,128)(2,1)S(1)}, bf16[1,1,2048,128]{3,2,1,0:T(8,128)(2,1)}, u32[]{:S(2)}) copy-start(bf16[1,1,2048,128]{3,2,1,0:T(8,128)(2,1)} %param.8) | copy-start | bytes 1572868
  40.0 3.6 %copy-start.3 = (bf16[1,4,512,512]{3,2,1,0:T(8,128)(2,1)S(1)}, bf16[1,4,512,512]{3,2,1,0:T(8,128)(2,1)}, u32[]{:S(2)}) copy-start(bf16[1,4,512,512]{3,2,1,0:T(8,128)(2,1)} %param.12) | copy-start | bytes 6291460
  55.2 8.8 %copy-start.6 = (bf16[1,512]{1,0:T(2,128)(2,1)S(1)}, bf16[1,512]{1,0:T(2,128)(2,1)}, u32[]{:S(2)}) copy-start(bf16[1,512]{1,0:T(2,128)(2,1)} %param.14) | copy-start | bytes 3076
  62.1 1.9 %copy-start.1 = (bf16[4096,512]{1,0:T(8,128)(2,1)}, bf16[4096,512]{1,0:T(8,128)(2,1)S(1)}, u32[]{:S(2)}) copy-start(bf16[4096,512]{1,0:T(8,128)(2,1)S(1)} %add_convert_fusion) | copy-start | bytes 12582916
  64.0 6.5 %copy-start.4 = (bf16[1,512,128]{2,1,0:T(8,128)(2,1)S(1)}, bf16[1,512,128]{2,1,0:T(8,128)(2,1)}, u32[]{:S(2)}) copy-start(bf16[1,512,128]{2,1,0:T(8,128)(2,1)} %param.13) | copy-start | bytes 393220
  67.1 8.0 %all-to-all-start.1 = ((bf16[4,2,512]{2,1,0:T(2,128)(2,1)}), bf16[4,2,512]{2,1,0:T(2,128)(2,1)S(1)}, u32[]{:S(2)}, u32[]{:S(2)}) async-start(bf16[4,2,512]{2,1,0:T(2,128)(2,1)} %reshape.161), calls=%async_computation.1 | async-start | bytes 16384 | tf_op jit(solution)/shard_map/all_to_all | solution.py:108
  70.5 9.0 %copy-start.2 = (bf16[3,3,3,128,128]{4,3,2,1,0:T(8,128)(2,1)S(1)}, bf16[3,3,3,128,128]{4,3,2,1,0:T(8,128)(2,1)}, u32[]{:S(2)}) copy-start(bf16[3,3,3,128,128]{4,3,2,1,0:T(8,128)(2,1)} %param.15) | copy-start | bytes 2654212
  75.0 17.7 %copy-start.5 = (s32[1,1,8,256]{3,2,1,0:T(8,128)S(1)}, s32[1,1,8,256]{3,2,1,0:T(8,128)}, u32[]{:S(2)}) copy-start(s32[1,1,8,256]{3,2,1,0:T(8,128)} %param.10) | copy-start | bytes 24580
  75.0 29.7 %all-to-all-start.2 = ((bf16[4,1024,128]{2,1,0:T(8,128)(2,1)}), bf16[4,1024,128]{2,1,0:T(8,128)(2,1)S(1)}, u32[]{:S(2)}, u32[]{:S(2)}) async-start(bf16[4,1024,128]{2,1,0:T(8,128)(2,1)} %bitcast.17), calls=%async_computation.2 | async-start | bytes 2097152 | tf_op jit(solution)/shard_map/all_to_all | solution.py:107
  111.3 2.6 %collective-permute-start = (bf16[16,3,128]{2,1,0:T(4,128)(2,1)S(1)}, bf16[16,3,128]{2,1,0:T(4,128)(2,1)S(1)}, u32[]{:S(2)}, u32[]{:S(2)}) collective-permute-start(bf16[16,3,128]{2,1,0:T(4,128)(2,1)S(1)} %get-tuple-element.10), channel_id=1, source_target_pairs={{0,4},{4,8},{8,12},{1,5},{5,9},{9,13},{2,6},{6,10},{10,14},{3,7},{... | collective-permute-start | bytes 36872 | tf_op jit(solution)/shard_map/ppermute | solution.py:20
  112.6 4.5 %collective-permute-start.1 = (bf16[16,3,128]{2,1,0:T(4,128)(2,1)S(1)}, bf16[16,3,128]{2,1,0:T(4,128)(2,1)S(1)}, u32[]{:S(2)}, u32[]{:S(2)}) collective-permute-start(bf16[16,3,128]{2,1,0:T(4,128)(2,1)S(1)} %get-tuple-element.11), channel_id=1, source_target_pairs={{4,0},{8,4},{12,8},{5,1},{9,5},{13,9},{6,2},{10,6},{14,10},{7,3},{... | collective-permute-start | bytes 36872 | tf_op jit(solution)/shard_map/ppermute | solution.py:21
  117.1 7.9 %collective-permute-start.2 = (bf16[3,22,128]{2,1,0:T(8,128)(2,1)S(1)}, bf16[3,22,128]{2,1,0:T(8,128)(2,1)S(1)}, u32[]{:S(2)}, u32[]{:S(2)}) collective-permute-start(bf16[3,22,128]{2,1,0:T(8,128)(2,1)S(1)} %get-tuple-element.8), channel_id=1, source_target_pairs={{0,1},{1,2},{2,3},{4,5},{5,6},{6,7},{8,9},{9,10},{10,11},{12,13},{... | collective-permute-start | bytes 50696 | tf_op jit(solution)/shard_map/ppermute | solution.py:20
  122.7 5.1 %collective-permute-start.3 = (bf16[3,22,128]{2,1,0:T(8,128)(2,1)S(1)}, bf16[3,22,128]{2,1,0:T(8,128)(2,1)S(1)}, u32[]{:S(2)}, u32[]{:S(2)}) collective-permute-start(bf16[3,22,128]{2,1,0:T(8,128)(2,1)S(1)} %get-tuple-element.9), channel_id=1, source_target_pairs={{1,0},{2,1},{3,2},{5,4},{6,5},{7,6},{9,8},{10,9},{11,10},{13,12},{... | collective-permute-start | bytes 50696 | tf_op jit(solution)/shard_map/ppermute | solution.py:21
where the time goes:
time: 132 us; the launch traced here: 131 us
  local copies, waits for them, and re-layouts  30.1 us (23%)
  blocking collectives  30.1 us (23%)
  matrix products  29.7 us (22%)
  starting transfers between devices  18 us (14%)
  waiting for transfers between devices  17.9 us (14%)
  other arithmetic  4.93 us (4%)
    all_to_all x1, blocking collectives, shards(): lax.all_to_all(sendbuf, 'blocks', split_axis=0, concat_axis=0, tiled=True)  30.1 us
    dot_general x4, matrix products, evaluate(): jnp.dot(hidden_act, hidden[layer_index], preferred_element_type=jnp.float32)  18.4 us
    gather x1, local copies, waits for them, and re-layouts, shards(): density_back.reshape(block_count * capacity)[slot_index]  13.1 us
    all_to_all x1, waiting for transfers between devices, shards(): lax.all_to_all(features, 'blocks', split_axis=0, concat_axis=0, tiled=True)  11.9 us
    ppermute x2, starting transfers between devices, with_halo(): before = lax.ppermute(last, axis, up)  6.9 us
    gather x1, local copies, waits for them, and re-layouts, shards(): feat_back.reshape(block_count * capacity, out_width)[slot_index]  6.18 us
    scatter x1, local copies, waits for them, and re-layouts, shards(): jnp.zeros((block_count * capacity, in_width), jnp.bfloat16).at[slot_index]  6.05 us
    ppermute x2, waiting for transfers between devices, with_halo(): after = lax.ppermute(initial, axis, down)  6 us
  transfers between devices with their start and end apart: 6, of which 3 were waited for; matrix products, arithmetic and copies ran while one was open for 14% of the time, Pallas kernels for 0%

commit v1 on v0

v1 whole, which is shorter than its diff:
```python
import functools

import jax
import jax.numpy as jnp
from jax import lax
from jax.experimental import pallas as pl
from jax.experimental.pallas import tpu as pltpu
from jax.sharding import PartitionSpec as P

SEGS_RAY = 8
CONV_LAYERS = 3
TW = 16
TH = 16
RAYS_DEV = 256
MESH = pl.DeviceIdType.MESH
F32 = jnp.float32
BF16 = jnp.bfloat16


def silu(value):
    half = 0.5 * value
    return half + half * jnp.tanh(half)


def softplus(value):
    return jnp.maximum(value, 0.0) + jnp.log1p(jnp.exp(-jnp.abs(value)))


def block_at(step, place, count):
    near = jnp.minimum(place, count - 1 - place)
    distance = (step + 1) // 2
    paired = jnp.where(step % 2 == 1, place + distance, place - distance)
    rest = jnp.where(2 * place <= count - 1, step, count - 1 - step)
    return jnp.where(step <= 2 * near, paired, rest)


Z, X, Y, D, SA, SX, SY, SD, ZD = range(9)


def render_kernel(
    count,
    capacity,
    row_tile,
    feat_ref,
    block_ref,
    rank_ref,
    w_in_ref,
    w_hid_ref,
    w_out_ref,
    w_dens_ref,
    color_ref,
    hid,
    ends,
    slot_row,
    slot_col,
    rank_col,
    act,
    heads,
    total,
    send_sem,
    recv_sem,
    ends_send,
    ends_recv,
    own_sem,
):
    place = lax.axis_index("blocks")
    tile = lax.axis_index("tiles")
    group = lax.axis_index("groups")
    core = lax.axis_index("sub")
    tile_mate = tile + 1 - 2 * (tile % 2)
    group_mate = group + 1 - 2 * (group % 2)
    core_mate = 1 - core
    tx, gy = tile % 2, group % 2
    layers = w_hid_ref.shape[0]
    hidden = w_hid_ref.shape[2]
    part = hidden // 8
    end_rows = ends.shape[1]
    end_half = end_rows // 2
    feats = w_out_ref.shape[1]
    in_width = w_in_ref.shape[0]
    segments = feat_ref.shape[0]

    def eighth(a, b, c):
        return (a * 2 + b) * 2 + c

    to_x, to_y, to_c = {"tiles": tile_mate}, {"groups": group_mate}, {"sub": core_mate}

    barrier = pltpu.get_barrier_semaphore()
    pl.semaphore_signal(barrier, inc=1, device_id=to_x, device_id_type=MESH)
    pl.semaphore_signal(barrier, inc=1, device_id=to_y, device_id_type=MESH)
    pl.semaphore_signal(barrier, inc=1, device_id=to_c, device_id_type=MESH)

    @pl.when(place > 0)
    def _():
        pl.semaphore_signal(barrier, inc=1, device_id={"blocks": place - 1}, device_id_type=MESH)

    @pl.when(place < count - 1)
    def _():
        pl.semaphore_signal(barrier, inc=1, device_id={"blocks": place + 1}, device_id_type=MESH)

    own = pltpu.make_async_copy(w_hid_ref, hid.at[place], own_sem)
    own.start()
    ends[place, 0:in_width] = w_in_ref[...]
    ends[place, in_width : in_width + feats] = w_out_ref[...].T
    ends[place, in_width + feats : end_rows] = jnp.broadcast_to(
        w_dens_ref[...], (end_rows - in_width - feats, hidden)
    )
    own.wait()

    peers = 3 + jnp.minimum(place, 1) + jnp.minimum(count - 1 - place, 1)
    pl.semaphore_wait(barrier, peers)

    def piece(block, layer, which):
        return hid.at[block, layer, pl.ds(pl.multiple_of(which * part, part), part)]

    def move(block, layer, which, kind, target, send_kind=None):
        ref = piece(block, layer, which)
        return pltpu.make_async_remote_copy(
            src_ref=ref,
            dst_ref=ref,
            send_sem=send_sem.at[block, layer, kind if send_kind is None else send_kind],
            recv_sem=recv_sem.at[block, layer, kind],
            device_id=target,
            device_id_type=MESH,
        )

    def move_ends(block, half, kind, target, send_kind=None):
        ref = ends.at[block, pl.ds(pl.multiple_of(half * end_half, end_half), end_half)]
        return pltpu.make_async_remote_copy(
            src_ref=ref,
            dst_ref=ref,
            send_sem=ends_send.at[block, kind if send_kind is None else send_kind],
            recv_sem=ends_recv.at[block, kind],
            device_id=target,
            device_id_type=MESH,
        )

    e_own = eighth(tx, gy, core)
    e_x = eighth(1 - tx, gy, core)
    e_y = eighth(tx, 1 - gy, core)
    e_d = eighth(1 - tx, 1 - gy, core)
    m_own = eighth(tx, gy, core_mate)
    m_x = eighth(1 - tx, gy, core_mate)
    m_y = eighth(tx, 1 - gy, core_mate)
    m_d = eighth(1 - tx, 1 - gy, core_mate)
    up, down = {"blocks": place + 1}, {"blocks": place - 1}

    def own_up(action):
        @pl.when(place < count - 1)
        def _():
            action(move_ends(place, core, 0, up))
            for layer in range(layers):
                action(move(place, layer, e_own, Z, up))

    def own_down(action):
        @pl.when(place > 0)
        def _():
            action(move_ends(place, core, 0, down, 2))
            for layer in range(layers):
                action(move(place, layer, e_own, Z, down, ZD))

    own_up(lambda c: c.start())
    own_down(lambda c: c.start())

    def onward(block, action):
        @pl.when((block < place) & (place < count - 1))
        def _():
            action(up)

        @pl.when((block > place) & (place > 0))
        def _():
            action(down)

    def arrive(block, layer):
        move(block, layer, e_own, Z, up).wait_recv()
        onward(block, lambda to: move(block, layer, e_own, Z, to).start())
        move(block, layer, e_own, X, to_x).start()
        move(block, layer, e_own, Y, to_y).start()
        move(block, layer, e_own, SA, to_c).start()

    def arrive_ends(block):
        move_ends(block, core, 0, up).wait_recv()
        onward(block, lambda to: move_ends(block, core, 0, to).start())
        move_ends(block, core, 1, to_c).start()

    def cross(block, layer):
        move(block, layer, e_x, X, to_x).wait_recv()
        move(block, layer, e_y, Y, to_y).wait_recv()

        @pl.when(core == 0)
        def _():
            move(block, layer, e_x, D, to_y).start()

        @pl.when(core == 1)
        def _():
            move(block, layer, e_y, D, to_x).start()

        move(block, layer, e_x, SX, to_c).start()
        move(block, layer, e_y, SY, to_c).start()

    def corner(block, layer):
        move(block, layer, e_d, D, to_x).wait_recv()
        move(block, layer, e_d, SD, to_c).start()

    def ready(block, layer):
        move(block, layer, m_own, SA, to_c).wait_recv()
        move(block, layer, m_x, SX, to_c).wait_recv()
        move(block, layer, m_y, SY, to_c).wait_recv()
        move(block, layer, m_d, SD, to_c).wait_recv()

    def item(step, layer, ahead):
        return step + (layer + ahead) // layers, (layer + ahead) % layers

    def exchange(step, layer):
        for ahead, action in ((3, arrive), (2, cross), (1, corner)):
            later, its_layer = item(step, layer, ahead)

            @pl.when((later > 0) & (later < count))
            def _():
                block = block_at(later, place, count)
                if action is arrive and its_layer == 0:
                    arrive_ends(block)
                action(block, its_layer)

    rows16 = 16
    lane = lax.broadcasted_iota(jnp.int32, (128, 128), 1)
    sub = lax.broadcasted_iota(jnp.int32, (128, 128), 0)
    earlier = (sub < lane).astype(F32).astype(BF16)
    names = lax.broadcasted_iota(jnp.int32, (rows16, 128), 0)
    base = names.astype(F32) * capacity
    carry = jnp.zeros((rows16, 1), F32)
    for chunk in range(segments // 128):
        cols = slice(chunk * 128, (chunk + 1) * 128)
        named = (jnp.broadcast_to(block_ref[:, cols], (rows16, 128)) == names).astype(F32)
        before = jnp.dot(named.astype(BF16), earlier, preferred_element_type=F32) + carry
        carry = carry + jnp.sum(named, axis=1, keepdims=True)
        slots = jnp.sum(named * (before + base), axis=0, keepdims=True)
        slot_row[:, cols] = slots.astype(jnp.int32)
        slot_col[cols, :] = jnp.broadcast_to(slots, (128, 128)).T.astype(jnp.int32)
    for k in range(SEGS_RAY):
        spread = jnp.broadcast_to(rank_ref[k : k + 1, :].astype(F32), (128, RAYS_DEV))
        rank_col[k] = spread.T
    total[...] = jnp.zeros_like(total)

    tiles_n = capacity // row_tile

    def tile_loop(body):
        def run(index, carry_in):
            body(pl.ds(pl.multiple_of(index * row_tile, row_tile), row_tile), index)
            return carry_in

        lax.fori_loop(0, tiles_n, run, 0)

    def gather_in(block):
        def body(rows, index):
            wanted = (
                lax.broadcasted_iota(jnp.int32, (row_tile, segments), 0)
                + block * capacity
                + index * row_tile
            )
            pick = (slot_row[...] == wanted).astype(F32).astype(BF16)
            mine = jnp.dot(pick, feat_ref[...], preferred_element_type=F32).astype(BF16)
            act[rows] = silu(
                jnp.dot(mine, ends[block, 0:in_width], preferred_element_type=F32)
            ).astype(BF16)

        tile_loop(body)

    def layer_step(block, layer):
        def body(rows, index):
            value = act[rows]
            update = silu(jnp.dot(value, hid[block, layer], preferred_element_type=F32))
            act[rows] = (value.astype(F32) + update).astype(BF16)

        tile_loop(body)

    def head_step(block):
        w_feat = ends[block, in_width : in_width + feats]
        w_den = jnp.broadcast_to(ends[block, in_width + feats : in_width + feats + 1], (128, hidden))
        contract = (((1,), (1,)), ((), ()))

        def body(rows, index):
            value = act[rows]
            heads[rows, 0:feats] = lax.dot_general(
                value, w_feat, contract, preferred_element_type=F32
            ).astype(BF16)
            raw = lax.dot_general(value, w_den, contract, preferred_element_type=F32)
            heads[rows, feats : feats + 128] = (0.25 * softplus(raw)).astype(BF16)

        tile_loop(body)

    def scatter_back(block):
        def run(index, carry_in):
            rows = pl.ds(pl.multiple_of(index * 256, 256), 256)
            held = slot_col[rows] - block * capacity
            columns = lax.broadcasted_iota(jnp.int32, (256, 128), 1)
            pick = jnp.concatenate(
                [
                    (held == columns + 128 * j).astype(F32).astype(BF16)
                    for j in range(capacity // 128)
                ],
                axis=1,
            )
            total[rows] += jnp.dot(pick, heads[...], preferred_element_type=F32)
            return carry_in

        lax.fori_loop(0, segments // 256, run, 0)

    def step_body(step, carry_in):
        block = block_at(step, place, count)
        for layer in range(layers):
            exchange(step, layer)

            @pl.when(step > 0)
            def _():
                if layer == 0:
                    move_ends(block, core_mate, 1, to_c).wait_recv()
                ready(block, layer)

            if layer == 0:
                gather_in(block)
            layer_step(block, layer)
        head_step(block)
        scatter_back(block)
        return carry_in

    lax.fori_loop(0, count, step_body, 0)

    density = [total[k * RAYS_DEV : (k + 1) * RAYS_DEV, feats : feats + 128] for k in range(SEGS_RAY)]
    color = jnp.zeros((RAYS_DEV, feats), F32)
    for k in range(SEGS_RAY):
        optical = jnp.zeros((RAYS_DEV, 128), F32)
        for j in range(SEGS_RAY):
            if j != k:
                optical += jnp.where(rank_col[j] < rank_col[k], density[j], 0.0)
        weight = jnp.exp(-optical) * (1.0 - jnp.exp(-density[k]))
        color += weight * total[k * RAYS_DEV : (k + 1) * RAYS_DEV, 0:feats]
    color_ref[...] = color.astype(BF16)

    own_up(lambda c: c.wait_send())
    own_down(lambda c: c.wait_send())

    def drain(step, carry_in):
        block = block_at(step, place, count)
        onward(block, lambda to: move_ends(block, core, 0, to).wait_send())
        move_ends(block, core, 1, to_c).wait_send()
        for layer in range(layers):
            onward(block, lambda to, layer=layer: move(block, layer, e_own, Z, to).wait_send())
            for kind in (X, Y, D, SA, SX, SY, SD):
                move(block, layer, e_own, kind, to_c).wait_send()
        return carry_in

    lax.fori_loop(1, count, drain, 0)


def render(count, rows, block_ids, ranks, w_in, w_hid, w_out, w_dens):
    segments, in_width = rows.shape
    capacity = 2 * segments // count
    layers, hidden, _ = w_hid.shape
    feats = w_out.shape[1]
    row_tile = min(512, capacity)
    end_rows = in_width + feats + 32
    vmem = pl.BlockSpec(memory_space=pltpu.VMEM)
    macs = count * capacity * hidden * (in_width + layers * hidden + feats)
    return pl.pallas_call(
        functools.partial(render_kernel, count, capacity, row_tile),
        out_shape=jax.ShapeDtypeStruct((RAYS_DEV, feats), BF16),
        in_specs=[vmem, vmem, vmem, vmem, pl.BlockSpec(memory_space=pl.ANY), vmem, vmem],
        out_specs=vmem,
        scratch_shapes=[
            pltpu.VMEM((count, layers, hidden, hidden), BF16),
            pltpu.VMEM((count, end_rows, hidden), BF16),
            pltpu.VMEM((1, segments), jnp.int32),
            pltpu.VMEM((segments, 128), jnp.int32),
            pltpu.VMEM((SEGS_RAY, RAYS_DEV, 128), F32),
            pltpu.VMEM((capacity, hidden), BF16),
            pltpu.VMEM((capacity, feats + 128), BF16),
            pltpu.VMEM((segments, feats + 128), F32),
            pltpu.SemaphoreType.DMA((count, layers, 9)),
            pltpu.SemaphoreType.DMA((count, layers, 8)),
            pltpu.SemaphoreType.DMA((count, 3)),
            pltpu.SemaphoreType.DMA((count, 2)),
            pltpu.SemaphoreType.DMA,
        ],
        compiler_params=pltpu.CompilerParams(
            collective_id=0, has_side_effects=True, vmem_limit_bytes=56 * 1024 * 1024
        ),
        cost_estimate=pl.CostEstimate(flops=2 * macs, bytes_accessed=4 << 20, transcendentals=0),
        name="render",
    )(rows, block_ids, ranks, w_in, w_hid, w_out, w_dens)


def with_halo(shard, sides, width):
    for axis, dim in sides:
        peers, length = (lax.axis_size(axis), shard.shape[dim])
        up = [(i, (i + 1) % peers) for i in range(peers - 1)]
        down = [(j, i) for i, j in up]
        last = lax.slice_in_dim(shard, length - width, length, axis=dim)
        initial = lax.slice_in_dim(shard, 0, width, axis=dim)
        before = lax.ppermute(last, axis, up)
        after = lax.ppermute(initial, axis, down)
        shard = jnp.concatenate([before, shard, after], axis=dim)
    return shard


def conv_layer(padded, kernel, out_rows, out_cols):
    pieces = []
    for offset_y in range(3):
        for offset_x in range(3):
            pieces.append(padded[offset_y : offset_y + out_rows, offset_x : offset_x + out_cols])
    patches = jnp.concatenate(pieces, axis=-1)
    channels = kernel.shape[-1]
    result = jnp.dot(
        patches, kernel.reshape(9 * kernel.shape[2], channels), preferred_element_type=jnp.float32
    )
    center = padded[1 : 1 + out_rows, 1 : 1 + out_cols].astype(jnp.float32)
    return (center + jax.nn.silu(result)).astype(jnp.bfloat16)


def shards(seg_feat, seg_block, depth_rank, w_in, w_hidden, w_out, w_dens, conv_w):
    block_count = lax.axis_size("blocks")
    segments = seg_feat.shape[2]
    color = render(
        block_count,
        seg_feat[0, 0],
        seg_block.reshape(1, segments),
        depth_rank[0, 0],
        w_in[0],
        w_hidden[0],
        w_out[0],
        w_dens,
    )
    tile_image = color.reshape(TH, TW, color.shape[1])
    rows_total = TH * lax.axis_size(("tiles", "sub"))
    cols_total = TW * block_count
    row_pos = (
        lax.axis_index(("tiles", "sub")) * TH
        - CONV_LAYERS
        + jnp.arange(TH + 2 * CONV_LAYERS, dtype=jnp.int32)
    )
    col_pos = (
        lax.axis_index("blocks") * TW
        - CONV_LAYERS
        + jnp.arange(TW + 2 * CONV_LAYERS, dtype=jnp.int32)
    )
    inside = ((row_pos >= 0) & (row_pos < rows_total))[:, None] & (
        (col_pos >= 0) & (col_pos < cols_total)
    )[None, :]
    current = with_halo(tile_image, (("blocks", 1), (("tiles", "sub"), 0)), CONV_LAYERS)
    for layer_index in range(CONV_LAYERS):
        margin = CONV_LAYERS - layer_index - 1
        size_h = TH + 2 * margin
        size_w = TW + 2 * margin
        current = conv_layer(current, conv_w[layer_index], size_h, size_w)
        keep_mask = inside[
            layer_index + 1 : layer_index + 1 + size_h, layer_index + 1 : layer_index + 1 + size_w
        ]
        current = jnp.where(keep_mask[:, :, None], current, jnp.zeros_like(current))
    tile_image = current
    return tile_image


def solution(mesh):
    in_specs = (
        P(("groups", "tiles", "sub"), "blocks", None, None),
        P(("groups", "tiles", "sub"), "blocks", None, None),
        P(("groups", "tiles", "sub"), "blocks", None, None),
        P("blocks", None, None),
        P("blocks", None, None, None),
        P("blocks", None, None),
        P("blocks", None),
        P(),
    )
    out_specs = P(("groups", "tiles", "sub"), "blocks", None)
    return jax.shard_map(shards, mesh=mesh, in_specs=in_specs, out_specs=out_specs, check_vma=False)
```

time: 132 us -> 98.4 us (0.75)
  Pallas kernels: 0 us -> 78.8 us
  blocking collectives: 30.1 us -> 0 us
  local copies, waits for them, and re-layouts: 30.1 us -> 2.24 us
  matrix products: 29.7 us -> 1.96 us
  waiting for transfers between devices: 17.9 us -> 5.92 us
  starting transfers between devices: 18 us -> 8.55 us
  other arithmetic: 4.93 us -> 0.16 us
    pallas_call x0 -> x1, Pallas kernels: none -> 78.8 us  [render(): pl.pallas_call(functools.partial(render_kernel, count, capacity, row_tile...]
    all_to_all x1 -> x0, blocking collectives: 30.1 us -> none  [shards(): lax.all_to_all(sendbuf, 'blocks', split_axis=0, concat_axis=0, tiled=True)]
    dot_general x7 -> x0, matrix products: 27.7 us -> none  [the longest x4 18.4 us: evaluate(): jnp.dot(hidden_act, hidden[layer_index], preferred_element_type=jnp.float32)]
    gather x2 -> x0, local copies, waits for them, and re-layouts: 19.3 us -> none  [the longest x1 13.1 us: shards(): density_back.reshape(block_count * capacity)[slot_index]]
    all_to_all x2 -> x0, waiting for transfers between devices: 11.9 us -> none  [the longest x1 11.9 us: shards(): lax.all_to_all(features, 'blocks', split_axis=0, concat_axis=0, tiled=True)]
    all_to_all x2 -> x0, starting transfers between devices: 7.87 us -> none  [the longest x1 4.44 us: shards(): lax.all_to_all(features, 'blocks', split_axis=0, concat_axis=0, tiled=True)]
    scatter x1 -> x0, local copies, waits for them, and re-layouts: 6.05 us -> none  [shards(): jnp.zeros((block_count * capacity, in_width), jnp.bfloat16).at[slot_index]]
    unnamed x41 -> x28, local copies, waits for them, and re-layouts: 3.53 us -> 0.96 us
  transfers between devices with their start and end apart: 6 -> 4, of which waited for: 3 -> 2; matrix products, arithmetic and copies ran while one was open for 14% -> 0% of each run, Pallas kernels for 0% -> 0%
where the time goes in v1:
time: 98.4 us; the launch traced here: 97.9 us
  Pallas kernels  78.8 us (80%)
  starting transfers between devices  8.55 us (9%)
  waiting for transfers between devices  5.92 us (6%)
  local copies, waits for them, and re-layouts  2.24 us (2%)
  matrix products  1.96 us (2%)
    pallas_call x1, Pallas kernels, render(): pl.pallas_call(functools.partial(render_kernel, count, capacity, row_tile...  78.8 us
    ppermute x2, waiting for transfers between devices, with_halo(): after = lax.ppermute(initial, axis, down)  5.91 us
    ppermute x2, starting transfers between devices, with_halo(): before = lax.ppermute(last, axis, up)  5.34 us
    ppermute x2, starting transfers between devices, with_halo(): after = lax.ppermute(initial, axis, down)  3.21 us
  transfers between devices with their start and end apart: 4, of which 2 were waited for; matrix products, arithmetic and copies ran while one was open for 0% of the time, Pallas kernels for 0%

profile of v1, /device:TPU:1, one launch (start us, length us, event | category | flops | bytes accessed | tf_op | source)
XLA Modules:
  0.0 97.9 jit_solution(8969520375038772818)
XLA Ops:
  0.0 78.8 %render.1 = bf16[256,128]{1,0:T(8,128)(2,1)} custom-call(bf16[2048,128]{1,0:T(8,128)(2,1)} %bitcast.29, s32[1,2048]{1,0:T(1,128)} %bitcast.32, s32[8,256]{1,0:T(8,128)} %bitcast.33, bf16[128,512]{1,0:T(8,128)(2,1)} %bitcast.30, bf16[4,512,512]{2,1,0:T(8,128)(2,1)} %bitcast.28, bf16[512,128]{1,0:T(8,128)(2,1)} %bitcast.31, bf16[1,512]{1,0:T(2,128)(2,1)} %w_dens_ref.1), custom_call_target="tpu_custom_call" | custom-call | flops 9663676416 | bytes 4194304 | tf_op jit(solution)/shard_map/render/pallas_call | solution.py:365
  78.8 0.8 fusion.3
  79.7 1.3 %collective-permute-start = (bf16[16,3,128]{2,1,0:T(4,128)(2,1)S(1)}, bf16[16,3,128]{2,1,0:T(4,128)(2,1)S(1)}, u32[]{:S(2)}, u32[]{:S(2)}) collective-permute-start(bf16[16,3,128]{2,1,0:T(4,128)(2,1)S(1)} %get-tuple-element.10), channel_id=1, source_target_pairs={{0,4},{4,8},{8,12},{1,5},{5,9},{9,13},{2,6},{6,10},{10,14},{3,7},{... | collective-permute-start | bytes 36872 | tf_op jit(solution)/shard_map/ppermute | solution.py:400
  81.0 1.3 %collective-permute-start.1 = (bf16[16,3,128]{2,1,0:T(4,128)(2,1)S(1)}, bf16[16,3,128]{2,1,0:T(4,128)(2,1)S(1)}, u32[]{:S(2)}, u32[]{:S(2)}) collective-permute-start(bf16[16,3,128]{2,1,0:T(4,128)(2,1)S(1)} %get-tuple-element.11), channel_id=1, source_target_pairs={{4,0},{8,4},{12,8},{5,1},{9,5},{13,9},{6,2},{10,6},{14,10},{7,3},{... | collective-permute-start | bytes 36872 | tf_op jit(solution)/shard_map/ppermute | solution.py:401
  82.3 0.1 fusion.2
  82.4 3.1 %collective-permute-done.1 = bf16[16,3,128]{2,1,0:T(4,128)(2,1)S(1)} collective-permute-done((bf16[16,3,128]{2,1,0:T(4,128)(2,1)S(1)}, bf16[16,3,128]{2,1,0:T(4,128)(2,1)S(1)}, u32[]{:S(2)}, u32[]{:S(2)}) %collective-permute-start.1) | collective-permute-done | bytes 12320 | tf_op jit(solution)/shard_map/ppermute | solution.py:401
  85.5 4.1 %collective-permute-start.2 = (bf16[3,22,128]{2,1,0:T(8,128)(2,1)S(1)}, bf16[3,22,128]{2,1,0:T(8,128)(2,1)S(1)}, u32[]{:S(2)}, u32[]{:S(2)}) collective-permute-start(bf16[3,22,128]{2,1,0:T(8,128)(2,1)S(1)} %get-tuple-element.8), channel_id=1, source_target_pairs={{0,1},{1,2},{2,3},{4,5},{5,6},{6,7},{8,9},{9,10},{10,11},{12,13},{... | collective-permute-start | bytes 50696 | tf_op jit(solution)/shard_map/ppermute | solution.py:400
  89.5 1.9 %collective-permute-start.3 = (bf16[3,22,128]{2,1,0:T(8,128)(2,1)S(1)}, bf16[3,22,128]{2,1,0:T(8,128)(2,1)S(1)}, u32[]{:S(2)}, u32[]{:S(2)}) collective-permute-start(bf16[3,22,128]{2,1,0:T(8,128)(2,1)S(1)} %get-tuple-element.9), channel_id=1, source_target_pairs={{1,0},{2,1},{3,2},{5,4},{6,5},{7,6},{9,8},{10,9},{11,10},{13,12},{... | collective-permute-start | bytes 50696 | tf_op jit(solution)/shard_map/ppermute | solution.py:401
  91.5 0.1 broadcast_and_fusion
  91.6 0.1 slice.153
  91.6 0.1 slice.152
  91.7 0.1 slice.151
  91.8 2.8 %collective-permute-done.3 = bf16[3,22,128]{2,1,0:T(8,128)(2,1)S(1)} collective-permute-done((bf16[3,22,128]{2,1,0:T(8,128)(2,1)S(1)}, bf16[3,22,128]{2,1,0:T(8,128)(2,1)S(1)}, u32[]{:S(2)}, u32[]{:S(2)}) %collective-permute-start.3) | collective-permute-done | bytes 16928 | tf_op jit(solution)/shard_map/ppermute | solution.py:401
  94.7 0.1 slice_dynamic-update-slice_fusion.6
  94.8 0.1 slice_dynamic-update-slice_fusion.5
  94.9 0.1 slice_dynamic-update-slice_fusion.16
  94.9 0.1 slice_dynamic-update-slice_fusion.3
  95.0 0.1 slice_dynamic-update-slice_fusion.1
  95.1 0.1 slice_dynamic-update-slice_fusion
  95.2 0.5 broadcast_select_fusion
  95.7 0.1 slice_dynamic-update-slice_fusion.14
  95.8 0.1 slice_dynamic-update-slice_fusion.13
  96.1 0.5 fusion
  96.9 1.0 fusion.1
  (28 shorter events, 0.8 us)
Async XLA Ops:
  0.0 82.3 %copy-start = (bf16[3,3,3,128,128]{4,3,2,1,0:T(8,128)(2,1)S(1)}, bf16[3,3,3,128,128]{4,3,2,1,0:T(8,128)(2,1)}, u32[]{:S(2)}) copy-start(bf16[3,3,3,128,128]{4,3,2,1,0:T(8,128)(2,1)} %param.15) | copy-start | bytes 2654212
  78.8 6.6 %copy-start.1 = (bf16[256,128]{1,0:T(8,128)(2,1)S(1)}, bf16[256,128]{1,0:T(8,128)(2,1)}, u32[]{:S(2)}) copy-start(bf16[256,128]{1,0:T(8,128)(2,1)} %render.1) | copy-start | bytes 196612
  79.7 2.7 %collective-permute-start = (bf16[16,3,128]{2,1,0:T(4,128)(2,1)S(1)}, bf16[16,3,128]{2,1,0:T(4,128)(2,1)S(1)}, u32[]{:S(2)}, u32[]{:S(2)}) collective-permute-start(bf16[16,3,128]{2,1,0:T(4,128)(2,1)S(1)} %get-tuple-element.10), channel_id=1, source_target_pairs={{0,4},{4,8},{8,12},{1,5},{5,9},{9,13},{2,6},{6,10},{10,14},{3,7},{... | collective-permute-start | bytes 36872 | tf_op jit(solution)/shard_map/ppermute | solution.py:400
  81.0 4.5 %collective-permute-start.1 = (bf16[16,3,128]{2,1,0:T(4,128)(2,1)S(1)}, bf16[16,3,128]{2,1,0:T(4,128)(2,1)S(1)}, u32[]{:S(2)}, u32[]{:S(2)}) collective-permute-start(bf16[16,3,128]{2,1,0:T(4,128)(2,1)S(1)} %get-tuple-element.11), channel_id=1, source_target_pairs={{4,0},{8,4},{12,8},{5,1},{9,5},{13,9},{6,2},{10,6},{14,10},{7,3},{... | collective-permute-start | bytes 36872 | tf_op jit(solution)/shard_map/ppermute | solution.py:401
  85.5 6.3 %collective-permute-start.2 = (bf16[3,22,128]{2,1,0:T(8,128)(2,1)S(1)}, bf16[3,22,128]{2,1,0:T(8,128)(2,1)S(1)}, u32[]{:S(2)}, u32[]{:S(2)}) collective-permute-start(bf16[3,22,128]{2,1,0:T(8,128)(2,1)S(1)} %get-tuple-element.8), channel_id=1, source_target_pairs={{0,1},{1,2},{2,3},{4,5},{5,6},{6,7},{8,9},{9,10},{10,11},{12,13},{... | collective-permute-start | bytes 50696 | tf_op jit(solution)/shard_map/ppermute | solution.py:400
  89.5 5.1 %collective-permute-start.3 = (bf16[3,22,128]{2,1,0:T(8,128)(2,1)S(1)}, bf16[3,22,128]{2,1,0:T(8,128)(2,1)S(1)}, u32[]{:S(2)}, u32[]{:S(2)}) collective-permute-start(bf16[3,22,128]{2,1,0:T(8,128)(2,1)S(1)} %get-tuple-element.9), channel_id=1, source_target_pairs={{1,0},{2,1},{3,2},{5,4},{6,5},{7,6},{9,8},{10,9},{11,10},{13,12},{... | collective-permute-start | bytes 50696 | tf_op jit(solution)/shard_map/ppermute | solution.py:401

commit v2 on v1

--- a/solution.py
+++ b/solution.py
@@ -52,11 +52,12 @@
     hid,
     ends,
     slot_row,
-    slot_col,
-    rank_col,
+    wide,
+    turns,
+    rays,
     act,
     heads,
-    total,
+    dens_map,
     send_sem,
     recv_sem,
     ends_send,
@@ -212,7 +213,7 @@
         return step + (layer + ahead) // layers, (layer + ahead) % layers
 
     def exchange(step, layer):
-        for ahead, action in ((3, arrive), (2, cross), (1, corner)):
+        for ahead, action in ((4, arrive), (3, cross), (2, corner)):
             later, its_layer = item(step, layer, ahead)
 
             @pl.when((later > 0) & (later < count))
@@ -236,22 +237,23 @@
         carry = carry + jnp.sum(named, axis=1, keepdims=True)
         slots = jnp.sum(named * (before + base), axis=0, keepdims=True)
         slot_row[:, cols] = slots.astype(jnp.int32)
-        slot_col[cols, :] = jnp.broadcast_to(slots, (128, 128)).T.astype(jnp.int32)
-    for k in range(SEGS_RAY):
-        spread = jnp.broadcast_to(rank_ref[k : k + 1, :].astype(F32), (128, RAYS_DEV))
-        rank_col[k] = spread.T
-    total[...] = jnp.zeros_like(total)
+    wide[:, 0:in_width] = feat_ref[...]
+    row_of = lax.broadcasted_iota(jnp.int32, (segments, 128), 0)
+    lane_of = lax.broadcasted_iota(jnp.int32, (segments, 128), 1)
+    ray, turn = row_of % RAYS_DEV, row_of // RAYS_DEV
+    tags = jnp.where(lane_of == SEGS_RAY, ray, jnp.where(lane_of == turn, 1, 0))
+    wide[:, in_width : in_width + 128] = tags.astype(F32).astype(BF16)
+    dens_map[...] = jnp.zeros_like(dens_map)
 
     tiles_n = capacity // row_tile
 
     def tile_loop(body):
-        def run(index, carry_in):
-            body(pl.ds(pl.multiple_of(index * row_tile, row_tile), row_tile), index)
-            return carry_in
-
-        lax.fori_loop(0, tiles_n, run, 0)
-
-    def gather_in(block):
+        for index in range(tiles_n):
+            body(slice(index * row_tile, (index + 1) * row_tile), index)
+
+    rows_first = (((0,), (0,)), ((), ()))
+
+    def gather_in(step, block):
         def body(rows, index):
             wanted = (
                 lax.broadcasted_iota(jnp.int32, (row_tile, segments), 0)
@@ -259,12 +261,22 @@
                 + index * row_tile
             )
             pick = (slot_row[...] == wanted).astype(F32).astype(BF16)
-            mine = jnp.dot(pick, feat_ref[...], preferred_element_type=F32).astype(BF16)
+            mine = jnp.dot(pick, wide[...], preferred_element_type=F32)
+            tag = mine[:, in_width : in_width + 128]
+            turns[step, rows] = jnp.where(lane_tile < SEGS_RAY, tag, 0.0).astype(BF16)
+            on_ray = lax.broadcasted_iota(jnp.int32, (row_tile, RAYS_DEV), 1).astype(F32)
+            rays[step, rows] = (tag[:, SEGS_RAY : SEGS_RAY + 1] == on_ray).astype(F32).astype(BF16)
             act[rows] = silu(
-                jnp.dot(mine, ends[block, 0:in_width], preferred_element_type=F32)
+                jnp.dot(
+                    mine[:, 0:in_width].astype(BF16),
+                    ends[block, 0:in_width],
+                    preferred_element_type=F32,
+                )
             ).astype(BF16)
 
         tile_loop(body)
+
+    lane_tile = lax.broadcasted_iota(jnp.int32, (row_tile, 128), 1)
 
     def layer_step(block, layer):
         def body(rows, index):
@@ -274,37 +286,20 @@
 
         tile_loop(body)
 
-    def head_step(block):
-        w_feat = ends[block, in_width : in_width + feats]
+    def head_step(step, block):
         w_den = jnp.broadcast_to(ends[block, in_width + feats : in_width + feats + 1], (128, hidden))
+        w_head = jnp.concatenate([ends[block, in_width : in_width + feats], w_den], axis=0)
         contract = (((1,), (1,)), ((), ()))
 
         def body(rows, index):
-            value = act[rows]
-            heads[rows, 0:feats] = lax.dot_general(
-                value, w_feat, contract, preferred_element_type=F32
-            ).astype(BF16)
-            raw = lax.dot_general(value, w_den, contract, preferred_element_type=F32)
-            heads[rows, feats : feats + 128] = (0.25 * softplus(raw)).astype(BF16)
+            out = lax.dot_general(act[rows], w_head, contract, preferred_element_type=F32)
+            heads[step, rows] = out[:, 0:feats].astype(BF16)
+            density = (0.25 * softplus(out[:, feats : feats + 128])).astype(BF16)
+            dens_map[...] += lax.dot_general(
+                turns[step, rows] * density, rays[step, rows], rows_first, preferred_element_type=F32
+            )
 
         tile_loop(body)
-
-    def scatter_back(block):
-        def run(index, carry_in):
-            rows = pl.ds(pl.multiple_of(index * 256, 256), 256)
-            held = slot_col[rows] - block * capacity
-            columns = lax.broadcasted_iota(jnp.int32, (256, 128), 1)
-            pick = jnp.concatenate(
-                [
-                    (held == columns + 128 * j).astype(F32).astype(BF16)
-                    for j in range(capacity // 128)
-                ],
-                axis=1,
-            )
-            total[rows] += jnp.dot(pick, heads[...], preferred_element_type=F32)
-            return carry_in
-
-        lax.fori_loop(0, segments // 256, run, 0)
 
     def step_body(step, carry_in):
         block = block_at(step, place, count)
@@ -318,24 +313,34 @@
                 ready(block, layer)
 
             if layer == 0:
-                gather_in(block)
+                gather_in(step, block)
             layer_step(block, layer)
-        head_step(block)
-        scatter_back(block)
+        head_step(step, block)
         return carry_in
 
     lax.fori_loop(0, count, step_body, 0)
 
-    density = [total[k * RAYS_DEV : (k + 1) * RAYS_DEV, feats : feats + 128] for k in range(SEGS_RAY)]
-    color = jnp.zeros((RAYS_DEV, feats), F32)
+    density = dens_map[0:SEGS_RAY]
+    optical = jnp.zeros((SEGS_RAY, RAYS_DEV), F32)
     for k in range(SEGS_RAY):
-        optical = jnp.zeros((RAYS_DEV, 128), F32)
-        for j in range(SEGS_RAY):
-            if j != k:
-                optical += jnp.where(rank_col[j] < rank_col[k], density[j], 0.0)
-        weight = jnp.exp(-optical) * (1.0 - jnp.exp(-density[k]))
-        color += weight * total[k * RAYS_DEV : (k + 1) * RAYS_DEV, 0:feats]
-    color_ref[...] = color.astype(BF16)
+        nearer = rank_ref[k : k + 1, :] < rank_ref[...]
+        optical += jnp.where(nearer, density[k : k + 1], 0.0)
+    weight = jnp.exp(-optical) * (1.0 - jnp.exp(-density))
+    weight = jnp.concatenate([weight, jnp.zeros((128 - SEGS_RAY, RAYS_DEV), F32)], axis=0)
+    coarse = weight.astype(BF16)
+    fine = (weight - coarse.astype(F32)).astype(BF16)
+
+    def blend(step, color):
+        turn_rows, ray_rows, head_rows = turns[step], rays[step], heads[step]
+        for share in (coarse, fine):
+            spread = jnp.dot(turn_rows, share, preferred_element_type=F32).astype(BF16) * ray_rows
+            color += lax.dot_general(
+                head_rows, spread, rows_first, preferred_element_type=F32
+            )
+        return color
+
+    color = lax.fori_loop(0, count, blend, jnp.zeros((feats, RAYS_DEV), F32))
+    color_ref[...] = color.T.astype(BF16)
 
     own_up(lambda c: c.wait_send())
     own_down(lambda c: c.wait_send())
@@ -371,11 +376,12 @@
             pltpu.VMEM((count, layers, hidden, hidden), BF16),
             pltpu.VMEM((count, end_rows, hidden), BF16),
             pltpu.VMEM((1, segments), jnp.int32),
-            pltpu.VMEM((segments, 128), jnp.int32),
-            pltpu.VMEM((SEGS_RAY, RAYS_DEV, 128), F32),
+            pltpu.VMEM((segments, in_width + 128), BF16),
+            pltpu.VMEM((count, capacity, 128), BF16),
+            pltpu.VMEM((count, capacity, RAYS_DEV), BF16),
             pltpu.VMEM((capacity, hidden), BF16),
-            pltpu.VMEM((capacity, feats + 128), BF16),
-            pltpu.VMEM((segments, feats + 128), F32),
+            pltpu.VMEM((count, capacity, feats), BF16),
+            pltpu.VMEM((128, RAYS_DEV), F32),
             pltpu.SemaphoreType.DMA((count, layers, 9)),
             pltpu.SemaphoreType.DMA((count, layers, 8)),
             pltpu.SemaphoreType.DMA((count, 3)),

time: 98.4 us -> 91 us (0.925)
  Pallas kernels: 78.8 us -> 70.9 us
    pallas_call x1, Pallas kernels: 78.8 us -> 70.9 us  [render(): pl.pallas_call(functools.partial(render_kernel, count, capacity, row_tile...]
where the time goes in v2:
time: 91 us; the launch traced here: 90.3 us
  Pallas kernels  70.9 us (78%)
  starting transfers between devices  8.91 us (10%)
  waiting for transfers between devices  5.92 us (7%)
  local copies, waits for them, and re-layouts  2.24 us (2%)
  matrix products  1.96 us (2%)
    pallas_call x1, Pallas kernels, render(): pl.pallas_call(functools.partial(render_kernel, count, capacity, row_tile...  70.9 us
    ppermute x2, waiting for transfers between devices, with_halo(): after = lax.ppermute(initial, axis, down)  5.91 us
    ppermute x2, starting transfers between devices, with_halo(): before = lax.ppermute(last, axis, up)  5.7 us
    ppermute x2, starting transfers between devices, with_halo(): after = lax.ppermute(initial, axis, down)  3.21 us
    dot_general x3, matrix products, conv_layer(): jnp.dot(patches, kernel.reshape(9 * kernel.shape[2], channels), preferred...  1.96 us
  transfers between devices with their start and end apart: 4, of which 2 were waited for; matrix products, arithmetic and copies ran while one was open for 0% of the time, Pallas kernels for 0%

profile of v2, /device:TPU:1, one launch (start us, length us, event | category | flops | bytes accessed | tf_op | source)
XLA Modules:
  0.0 90.3 jit_solution(12432830145135487406)
XLA Ops:
  0.0 70.9 %render.1 = bf16[256,128]{1,0:T(8,128)(2,1)} custom-call(bf16[2048,128]{1,0:T(8,128)(2,1)} %bitcast.29, s32[1,2048]{1,0:T(1,128)} %bitcast.32, s32[8,256]{1,0:T(8,128)} %bitcast.33, bf16[128,512]{1,0:T(8,128)(2,1)} %bitcast.30, bf16[4,512,512]{2,1,0:T(8,128)(2,1)} %bitcast.28, bf16[512,128]{1,0:T(8,128)(2,1)} %bitcast.31, bf16[1,512]{1,0:T(2,128)(2,1)} %w_dens_ref.1), custom_call_target="tpu_custom_call" | custom-call | flops 9663676416 | bytes 4194304 | tf_op jit(solution)/shard_map/render/pallas_call | solution.py:370
  71.0 0.8 fusion.3
  71.8 1.3 %collective-permute-start = (bf16[16,3,128]{2,1,0:T(4,128)(2,1)S(1)}, bf16[16,3,128]{2,1,0:T(4,128)(2,1)S(1)}, u32[]{:S(2)}, u32[]{:S(2)}) collective-permute-start(bf16[16,3,128]{2,1,0:T(4,128)(2,1)S(1)} %get-tuple-element.10), channel_id=1, source_target_pairs={{0,4},{4,8},{8,12},{1,5},{5,9},{9,13},{2,6},{6,10},{10,14},{3,7},{... | collective-permute-start | bytes 36872 | tf_op jit(solution)/shard_map/ppermute | solution.py:406
  73.1 1.3 %collective-permute-start.1 = (bf16[16,3,128]{2,1,0:T(4,128)(2,1)S(1)}, bf16[16,3,128]{2,1,0:T(4,128)(2,1)S(1)}, u32[]{:S(2)}, u32[]{:S(2)}) collective-permute-start(bf16[16,3,128]{2,1,0:T(4,128)(2,1)S(1)} %get-tuple-element.11), channel_id=1, source_target_pairs={{4,0},{8,4},{12,8},{5,1},{9,5},{13,9},{6,2},{10,6},{14,10},{7,3},{... | collective-permute-start | bytes 36872 | tf_op jit(solution)/shard_map/ppermute | solution.py:407
  74.4 0.1 fusion.2
  74.5 3.1 %collective-permute-done.1 = bf16[16,3,128]{2,1,0:T(4,128)(2,1)S(1)} collective-permute-done((bf16[16,3,128]{2,1,0:T(4,128)(2,1)S(1)}, bf16[16,3,128]{2,1,0:T(4,128)(2,1)S(1)}, u32[]{:S(2)}, u32[]{:S(2)}) %collective-permute-start.1) | collective-permute-done | bytes 12320 | tf_op jit(solution)/shard_map/ppermute | solution.py:407
  77.6 4.4 %collective-permute-start.2 = (bf16[3,22,128]{2,1,0:T(8,128)(2,1)S(1)}, bf16[3,22,128]{2,1,0:T(8,128)(2,1)S(1)}, u32[]{:S(2)}, u32[]{:S(2)}) collective-permute-start(bf16[3,22,128]{2,1,0:T(8,128)(2,1)S(1)} %get-tuple-element.8), channel_id=1, source_target_pairs={{0,1},{1,2},{2,3},{4,5},{5,6},{6,7},{8,9},{9,10},{10,11},{12,13},{... | collective-permute-start | bytes 50696 | tf_op jit(solution)/shard_map/ppermute | solution.py:406
  82.0 1.9 %collective-permute-start.3 = (bf16[3,22,128]{2,1,0:T(8,128)(2,1)S(1)}, bf16[3,22,128]{2,1,0:T(8,128)(2,1)S(1)}, u32[]{:S(2)}, u32[]{:S(2)}) collective-permute-start(bf16[3,22,128]{2,1,0:T(8,128)(2,1)S(1)} %get-tuple-element.9), channel_id=1, source_target_pairs={{1,0},{2,1},{3,2},{5,4},{6,5},{7,6},{9,8},{10,9},{11,10},{13,12},{... | collective-permute-start | bytes 50696 | tf_op jit(solution)/shard_map/ppermute | solution.py:407
  83.9 0.1 broadcast_and_fusion
  84.0 0.1 slice.153
  84.1 0.1 slice.152
  84.2 0.1 slice.151
  84.3 2.8 %collective-permute-done.3 = bf16[3,22,128]{2,1,0:T(8,128)(2,1)S(1)} collective-permute-done((bf16[3,22,128]{2,1,0:T(8,128)(2,1)S(1)}, bf16[3,22,128]{2,1,0:T(8,128)(2,1)S(1)}, u32[]{:S(2)}, u32[]{:S(2)}) %collective-permute-start.3) | collective-permute-done | bytes 16928 | tf_op jit(solution)/shard_map/ppermute | solution.py:407
  87.2 0.1 slice_dynamic-update-slice_fusion.6
  87.2 0.1 slice_dynamic-update-slice_fusion.5
  87.3 0.1 slice_dynamic-update-slice_fusion.16
  87.4 0.1 slice_dynamic-update-slice_fusion.3
  87.5 0.1 slice_dynamic-update-slice_fusion.1
  87.6 0.1 slice_dynamic-update-slice_fusion
  87.6 0.5 broadcast_select_fusion
  88.2 0.1 slice_dynamic-update-slice_fusion.14
  88.2 0.1 slice_dynamic-update-slice_fusion.13
  88.6 0.5 fusion
  89.4 1.0 %fusion.1 = bf16[16,16,128]{2,1,0:T(8,128)(2,1)} fusion(bf16[16,16,1152]{2,1,0:T(8,128)(2,1)S(1)} %slice_dynamic-update-slice_fusion.18, bf16[1152,128,1]{1,0,2:T(8,128)(2,1)S(1)} %bitcast.25, pred[16,16]{1,0:T(8,128)(4,1)S(1)} %slice.151, bf16[18,18,128]{2,1,0:T(8,128)(2,1)S(1)} %fusion), kind=kOutput, calls=%fused_computation.5 | convolution fusion | flops 75759616 | bytes 1016064 | tf_op jit(solution)/shard_map/dot_general | solution.py:419
  (28 shorter events, 0.8 us)
Async XLA Ops:
  0.0 74.4 %copy-start = (bf16[3,3,3,128,128]{4,3,2,1,0:T(8,128)(2,1)S(1)}, bf16[3,3,3,128,128]{4,3,2,1,0:T(8,128)(2,1)}, u32[]{:S(2)}) copy-start(bf16[3,3,3,128,128]{4,3,2,1,0:T(8,128)(2,1)} %param.15) | copy-start | bytes 2654212
  70.9 6.6 %copy-start.1 = (bf16[256,128]{1,0:T(8,128)(2,1)S(1)}, bf16[256,128]{1,0:T(8,128)(2,1)}, u32[]{:S(2)}) copy-start(bf16[256,128]{1,0:T(8,128)(2,1)} %render.1) | copy-start | bytes 196612
  71.8 2.7 %collective-permute-start = (bf16[16,3,128]{2,1,0:T(4,128)(2,1)S(1)}, bf16[16,3,128]{2,1,0:T(4,128)(2,1)S(1)}, u32[]{:S(2)}, u32[]{:S(2)}) collective-permute-start(bf16[16,3,128]{2,1,0:T(4,128)(2,1)S(1)} %get-tuple-element.10), channel_id=1, source_target_pairs={{0,4},{4,8},{8,12},{1,5},{5,9},{9,13},{2,6},{6,10},{10,14},{3,7},{... | collective-permute-start | bytes 36872 | tf_op jit(solution)/shard_map/ppermute | solution.py:406
  73.1 4.5 %collective-permute-start.1 = (bf16[16,3,128]{2,1,0:T(4,128)(2,1)S(1)}, bf16[16,3,128]{2,1,0:T(4,128)(2,1)S(1)}, u32[]{:S(2)}, u32[]{:S(2)}) collective-permute-start(bf16[16,3,128]{2,1,0:T(4,128)(2,1)S(1)} %get-tuple-element.11), channel_id=1, source_target_pairs={{4,0},{8,4},{12,8},{5,1},{9,5},{13,9},{6,2},{10,6},{14,10},{7,3},{... | collective-permute-start | bytes 36872 | tf_op jit(solution)/shard_map/ppermute | solution.py:407
  77.6 6.7 %collective-permute-start.2 = (bf16[3,22,128]{2,1,0:T(8,128)(2,1)S(1)}, bf16[3,22,128]{2,1,0:T(8,128)(2,1)S(1)}, u32[]{:S(2)}, u32[]{:S(2)}) collective-permute-start(bf16[3,22,128]{2,1,0:T(8,128)(2,1)S(1)} %get-tuple-element.8), channel_id=1, source_target_pairs={{0,1},{1,2},{2,3},{4,5},{5,6},{6,7},{8,9},{9,10},{10,11},{12,13},{... | collective-permute-start | bytes 50696 | tf_op jit(solution)/shard_map/ppermute | solution.py:406
  82.0 5.1 %collective-permute-start.3 = (bf16[3,22,128]{2,1,0:T(8,128)(2,1)S(1)}, bf16[3,22,128]{2,1,0:T(8,128)(2,1)S(1)}, u32[]{:S(2)}, u32[]{:S(2)}) collective-permute-start(bf16[3,22,128]{2,1,0:T(8,128)(2,1)S(1)} %get-tuple-element.9), channel_id=1, source_target_pairs={{1,0},{2,1},{3,2},{5,4},{6,5},{7,6},{9,8},{10,9},{11,10},{13,12},{... | collective-permute-start | bytes 50696 | tf_op jit(solution)/shard_map/ppermute | solution.py:407
